TPU v7x, 256 devices: a whole 4x4x8 slice. The times are simulated.
256 devices in a mesh: dp: 32 (over z, y), head: 8 (over x, core).
Axes of the slice: x: 4, y: 4, z: 8, core: 2. Of those that a mesh axis runs over, the one named last changes fastest.
Arguments:
- memory: bfloat16 [61440, 2048], P('dp'), may hold values from -6 to 6
- block_route: int32 [2, 480], P(None, 'dp'), may hold values from 0 to 31, as said below
- enc_len: int32 [192], P('dp'), may hold values from 1 to 512, as said below
- w_key: bfloat16 [2048, 2048], P(None, 'head'), may hold values from -0.125 to 0.125
- w_value: bfloat16 [2048, 2048], P(None, 'head'), may hold values from -0.125 to 0.125
- dec_query: bfloat16 [192, 2048], P('dp', 'head'), may hold values from -60 to 60
- dec_hidden: bfloat16 [192, 2048], P('dp', 'head'), may hold values from -1.5 to 1.5
- w_out: bfloat16 [2048, 2048], P('head'), may hold values from -0.125 to 0.125
Outputs:
- new_hidden: bfloat16 [192, 2048], P('dp', 'head')
- key_grid: bfloat16 [192, 512, 2048], P('dp', None, 'head')
- value_grid: bfloat16 [192, 512, 2048], P('dp', None, 'head')
Inputs may be any that keep to these rules, and one draw needn't show every extreme that they name: `enc_len`: request i belongs to home group i // 6. It has n_i = ceil(enc_len_i / 128) blocks, 1 to 4; the blocks of each home group sum to 30 minus those of its paired group, and every request has a request with 4 full blocks in its pair of groups. `block_route`: each home group's used cells (r * 4 + b with b < n of request r) appear exactly once over all slots, other cells never. Each slot holds 15 blocks and sends at most 1 of them to one home group; some slot sends exactly 1 to some group.
All inputs are finite; a program needn't handle non-finite values.
Results may differ from a plain program's by a relative error of at most 0.012.
The roundings to bfloat16 on the way count: a program that leaves them out, or rounds other values in their place, can miss the bound.
Values may be sent and summed in bfloat16 or wider, within the bound.
A program may use at most 128 MiB of HBM per device.

v0:
```python
import jax
import jax.numpy as jnp
from jax import lax
from jax.sharding import PartitionSpec as P

HEAD_DIM = 64
BLOCK = 128
MAXB = 4


def shards(memory, block_route, enc_len, w_key, w_value, dec_query, dec_hidden, w_out):
    peer_count = lax.axis_size("dp")
    req_count = enc_len.shape[0]
    grid_size = req_count * MAXB
    span = MAXB * BLOCK
    capacity = -(-grid_size // peer_count)
    slot_count = block_route.shape[1]
    home_ids = block_route[0]
    grid_cells = block_route[1]
    positions = jnp.arange(slot_count)
    earlier = (home_ids[:, None] == home_ids[None, :]) & (positions[None, :] < positions[:, None])
    slot_rank = jnp.sum(earlier.astype(jnp.int32), axis=1)
    targets = home_ids * capacity + slot_rank
    block_tags = (
        jnp.full((peer_count * capacity,), grid_size, jnp.int32).at[targets].set(grid_cells)
    )
    block_tags = block_tags.reshape(peer_count, capacity)
    columns = memory.shape[1]
    blocks = memory.reshape(slot_count, BLOCK, columns)
    buffer = (
        jnp.zeros((peer_count * capacity, BLOCK, columns), memory.dtype).at[targets].set(blocks)
    )
    memory_buffer = lax.all_to_all(buffer, "dp", split_axis=0, concat_axis=0, tiled=True)
    arrived = lax.all_to_all(block_tags, "dp", split_axis=0, concat_axis=0, tiled=True)
    columns = memory_buffer.shape[2]
    blocks = memory_buffer
    home_grid = (
        jnp.zeros((grid_size + 1, BLOCK, columns), memory_buffer.dtype)
        .at[arrived.reshape(-1)]
        .set(blocks)
    )
    flat_rows = home_grid[:grid_size].reshape(grid_size * BLOCK, columns)
    key_flat = jnp.dot(flat_rows, w_key, preferred_element_type=jnp.float32).astype(jnp.bfloat16)
    value_flat = jnp.dot(flat_rows, w_value, preferred_element_type=jnp.float32).astype(
        jnp.bfloat16
    )
    local_cols = w_key.shape[1]
    local_heads = local_cols // HEAD_DIM
    key_grid = key_flat.reshape(req_count, span, local_heads, HEAD_DIM)
    value_grid = value_flat.reshape(req_count, span, local_heads, HEAD_DIM)
    queries = dec_query.reshape(req_count, local_heads, HEAD_DIM)
    scores = jnp.einsum("rhd,rshd->rhs", queries, key_grid, preferred_element_type=jnp.float32)
    is_valid = jnp.arange(span)[None, None, :] < enc_len[:, None, None]
    scores = jnp.where(is_valid, scores, -1e30)
    peak = jnp.max(scores, axis=2, keepdims=True)
    expo = jnp.exp(scores - peak)
    attention = (expo / jnp.sum(expo, axis=2, keepdims=True)).astype(jnp.bfloat16)
    context = jnp.einsum("rhs,rshd->rhd", attention, value_grid, preferred_element_type=jnp.float32)
    context = context.astype(jnp.bfloat16).reshape(req_count, local_cols)
    partial_out = jnp.dot(context, w_out, preferred_element_type=jnp.float32)
    summed = lax.psum_scatter(partial_out, "head", scatter_dimension=1, tiled=True)
    new_hidden = (dec_hidden.astype(jnp.float32) + summed).astype(jnp.bfloat16)
    return (
        new_hidden,
        key_flat.reshape(req_count, span, local_cols),
        value_flat.reshape(req_count, span, local_cols),
    )


def solution(mesh):
    in_specs = (
        P("dp", None),
        P(None, "dp"),
        P("dp"),
        P(None, "head"),
        P(None, "head"),
        P("dp", "head"),
        P("dp", "head"),
        P("head", None),
    )
    out_specs = (P("dp", "head"), P("dp", None, "head"), P("dp", None, "head"))
    return jax.shard_map(shards, mesh=mesh, in_specs=in_specs, out_specs=out_specs, check_vma=False)
```

profile of v0, /device:TPU:1, one launch (start us, length us, event | category | flops | bytes accessed | tf_op | source)
XLA Modules:
  0.0 583.6 jit_solution(2486291949588800268)
XLA Ops:
  7.2 0.0 copy-start
  7.2 0.8 slice_bitcast_fusion
  8.0 0.2 convert_reduce_fusion
  8.2 0.7 fusion.16
  8.8 0.6 scatter_custom_fusion
  9.5 0.7 copy.19
  10.2 12.0 %all-to-all-start = ((s32[32,1,1]{2,1,0:T(1,128)}), s32[32,1,1]{2,1,0:T(1,128)S(1)}, u32[]{:S(2)}, u32[]{:S(2)}) async-start(s32[32,1,1]{2,1,0:T(1,128)} %copy.19), calls=%async_computation | async-start | bytes 32768 | tf_op jit(solution)/shard_map/all_to_all | solution.py:34
  22.2 6.0 %broadcast_in_dim.33 = bf16[32,128,2048]{2,1,0:T(8,128)(2,1)} broadcast(bf16[]{:T(256)} %constant.8.clone.1), dimensions={} | broadcast | bytes 16777218 | tf_op jit(solution)/shard_map/broadcast_in_dim | solution.py:31
  28.2 21.0 %scatter_fusion = bf16[32,128,2048]{2,1,0:T(8,128)(2,1)} fusion(bf16[32,128,2048]{2,1,0:T(8,128)(2,1)} %broadcast_in_dim.33, s32[15]{0:T(128)S(1)} %fusion.16, bf16[15,128,2048]{2,1,0:T(8,128)(2,1)} %bitcast.41), kind=kCustom, calls=%fused_computation.1 | custom fusion | bytes 23593020 | tf_op jit(solution)/shard_map/scatter | solution.py:31
  49.1 0.0 copy-start.4
  49.1 0.0 copy-start.6
  49.1 0.0 all-to-all-done
  49.1 9.5 %all-to-all-start.1 = ((bf16[32,128,2048]{2,1,0:T(8,128)(2,1)}), bf16[32,128,2048]{2,1,0:T(8,128)(2,1)}, u32[]{:S(2)}, u32[]{:S(2)}) async-start(bf16[32,128,2048]{2,1,0:T(8,128)(2,1)} %scatter_fusion), calls=%async_computation.1 | async-start | bytes 33554432 | tf_op jit(solution)/shard_map/all_to_all | solution.py:33
  58.7 0.0 reduce-scatter.2.cloned.1.call-start
  58.7 0.0 copy-done.4
  58.7 0.1 reshape.147
  58.8 0.0 copy-done.6
  58.8 0.1 iota_compare_fusion
  58.9 0.7 reduce
  59.6 371.6 %all-to-all-done.1 = bf16[32,128,2048]{2,1,0:T(8,128)(2,1)} async-done(((bf16[32,128,2048]{2,1,0:T(8,128)(2,1)}), bf16[32,128,2048]{2,1,0:T(8,128)(2,1)}, u32[]{:S(2)}, u32[]{:S(2)}) %all-to-all-start.1) | async-done | bytes 16777248 | tf_op jit(solution)/shard_map/all_to_all | solution.py:33
  431.2 6.3 %broadcast_in_dim.19 = bf16[25,128,2048]{2,1,0:T(8,128)(2,1)} broadcast(bf16[]{:T(256)} %constant.8.clone.1), dimensions={} | broadcast | bytes 13107202 | tf_op jit(solution)/shard_map/broadcast_in_dim | solution.py:38
  437.5 41.8 %scatter_fusion.1 = bf16[25,128,2048]{2,1,0:T(8,128)(2,1)} fusion(bf16[25,128,2048]{2,1,0:T(8,128)(2,1)} %broadcast_in_dim.19, s32[32]{0:T(128)S(1)} %fusion.17, bf16[32,128,2048]{2,1,0:T(8,128)(2,1)} %all-to-all-done.1), kind=kCustom, calls=%fused_computation.2 | custom fusion | bytes 50331776 | tf_op jit(solution)/shard_map/scatter | solution.py:40
  479.3 6.4 %slice.12 = bf16[24,128,2048]{2,1,0:T(8,128)(2,1)S(1)} slice(bf16[25,128,2048]{2,1,0:T(8,128)(2,1)} %scatter_fusion.1), slice={[0:24], [0:128], [0:2048]} | slice | bytes 25165824 | tf_op jit(solution)/shard_map/slice | solution.py:42
  485.7 0.0 copy-start.1
  485.8 4.6 copy-done.1
  490.3 0.0 copy-done
  490.3 3.6 convolution_convert_fusion.1
  493.9 0.0 copy-start.2
  494.0 3.0 reshape.145
  496.9 9.4 %convolution_convert_fusion = bf16[3072,256]{1,0:T(8,128)(2,1)} fusion(bf16[3072,2048]{1,0:T(8,128)(2,1)} %bitcast.40, bf16[2048,256]{1,0:T(8,128)(2,1)} %param.12), kind=kOutput, calls=%fused_computation.5 | convolution fusion | flops 3222011904 | bytes 15204352 | tf_op jit(solution)/shard_map/dot_general | solution.py:44
  506.3 0.0 copy-done.2
  506.3 0.0 copy-start.5
  506.3 5.8 reshape.148
  512.1 0.0 copy-start.3
  512.1 2.9 fusion.4
  515.0 0.2 fusion.10
  515.2 2.4 fusion.2
  517.6 0.1 reshape.114
  517.7 0.0 copy-done.3
  517.7 0.9 fusion.21
  518.6 0.0 reduce-scatter.2.cloned.1.call-update
  518.6 56.9 %reduce-scatter.2.cloned.1.call-done = f32[6,256]{1,0:T(8,128)} async-done(((f32[6,2048]{1,0:T(8,128)}), f32[6,256]{1,0:T(8,128)}) %reduce-scatter.2.cloned.1.call-update) | async-done | bytes 6160 | tf_op jit(solution)/shard_map/reduce_scatter | solution.py:61
  575.5 0.0 copy-done.5
  575.5 1.3 add_convert_fusion
  (2 shorter events, 0.0 us)
Async XLA Ops:
  7.2 483.2 %copy-start = (bf16[2048,256]{1,0:T(8,128)(2,1)S(1)}, bf16[2048,256]{1,0:T(8,128)(2,1)}, u32[]{:S(2)}) copy-start(bf16[2048,256]{1,0:T(8,128)(2,1)} %param.11) | copy-start | bytes 3145732
  10.2 39.0 %all-to-all-start = ((s32[32,1,1]{2,1,0:T(1,128)}), s32[32,1,1]{2,1,0:T(1,128)S(1)}, u32[]{:S(2)}, u32[]{:S(2)}) async-start(s32[32,1,1]{2,1,0:T(1,128)} %copy.19), calls=%async_computation | async-start | bytes 32768 | tf_op jit(solution)/shard_map/all_to_all | solution.py:34
  49.1 9.6 %copy-start.4 = (bf16[6,256]{1,0:T(8,128)(2,1)S(1)}, bf16[6,256]{1,0:T(8,128)(2,1)}, u32[]{:S(2)}) copy-start(bf16[6,256]{1,0:T(8,128)(2,1)} %param.13) | copy-start | bytes 9220
  49.1 9.7 %copy-start.6 = (s32[6]{0:T(128)S(1)}, s32[6]{0:T(128)}, u32[]{:S(2)}) copy-start(s32[6]{0:T(128)} %param.10) | copy-start | bytes 76
  49.1 382.0 %all-to-all-start.1 = ((bf16[32,128,2048]{2,1,0:T(8,128)(2,1)}), bf16[32,128,2048]{2,1,0:T(8,128)(2,1)}, u32[]{:S(2)}, u32[]{:S(2)}) async-start(bf16[32,128,2048]{2,1,0:T(8,128)(2,1)} %scatter_fusion), calls=%async_computation.1 | async-start | bytes 33554432 | tf_op jit(solution)/shard_map/all_to_all | solution.py:33
  58.7 516.8 %reduce-scatter.2.cloned.1.call-start = ((), (), s32[]{:S(2)}) async-start(), calls=%async_computation.3 | async-start | bytes 73728 | tf_op jit(solution)/shard_map/reduce_scatter | solution.py:61
  485.7 4.6 copy-start.1
  493.9 12.4 %copy-start.2 = (bf16[3072,256]{1,0:T(8,128)(2,1)}, bf16[3072,256]{1,0:T(8,128)(2,1)S(1)}, u32[]{:S(2)}) copy-start(bf16[3072,256]{1,0:T(8,128)(2,1)S(1)} %convolution_convert_fusion.1) | copy-start | bytes 4718596
  506.3 69.2 %copy-start.5 = (bf16[6,256]{1,0:T(8,128)(2,1)S(1)}, bf16[6,256]{1,0:T(8,128)(2,1)}, u32[]{:S(2)}) copy-start(bf16[6,256]{1,0:T(8,128)(2,1)} %param.14) | copy-start | bytes 9220
  512.1 5.6 copy-start.3
Sparse Core Ops, SparseCore 0:
  518.7 56.7 reduce-scatter.1
where the time goes:
time: 586 us; the launch traced here: 584 us
  waiting for transfers between devices  429 us (73%)
  local copies, waits for them, and re-layouts  97.1 us (17%)
  starting transfers between devices  21.6 us (4%)
  matrix products  19.2 us (3%)
  between operations  14.1 us (2%)
    all_to_all x1, waiting for transfers between devices, shards(): lax.all_to_all(buffer, 'dp', split_axis=0, concat_axis=0, tiled=True)  372 us
    reduce_scatter x1, waiting for transfers between devices, shards(): lax.psum_scatter(partial_out, 'head', scatter_dimension=1, tiled=True)  56.9 us
    scatter x1, local copies, waits for them, and re-layouts, shards(): home_grid = jnp.zeros((grid_size + 1, BLOCK, columns), memory_buffer.dtyp...  41.8 us
    scatter x1, local copies, waits for them, and re-layouts, shards(): jnp.zeros((peer_count * capacity, BLOCK, columns), memory.dtype).at[targets]  21 us
    all_to_all x1, starting transfers between devices, shards(): lax.all_to_all(block_tags, 'dp', split_axis=0, concat_axis=0, tiled=True)  12 us
  transfers between devices with their start and end apart: 3, of which 2 were waited for; matrix products, arithmetic and copies ran while one was open for 5% of the time, Pallas kernels for 0%

commit v1 on v0

v1 whole, which is shorter than its diff:
```python
import functools

import jax
import jax.numpy as jnp
from jax import lax
from jax.experimental import pallas as pl
from jax.experimental.pallas import tpu as pltpu
from jax.sharding import PartitionSpec as P

HEAD_DIM = 64
BLOCK = 128
MAXB = 4
ZN, YN, XN, CN = 8, 4, 4, 2
NDP, NHEAD = ZN * YN, XN * CN
RM = 112
RK = BLOCK - RM
GROUP = 2
NGROUP = NDP // GROUP
LAG = 2
MESH = pl.DeviceIdType.MESH
BF16 = jnp.bfloat16


def slot_offset(k):
    i, j = k // YN, k % YN
    dz = (i % 2) * ((i + 1) // 2) + (1 - i % 2) * ((ZN - i // 2) % ZN)
    dy = (j % 2) * ((j + 1) // 2) + (1 - j % 2) * ((YN - j // 2) % YN)
    return dz, dy


def move_kernel(
    table, mem, wk, wv, kv_mem, kv_dir, tags,
    own, rest, rest_kv, wts, packed, kv_out, tag_out, pool,
    in_sem, a_send, a_recv, d_send, d_recv, t_send, t_recv,
    xp_send, xp_recv, xm_send, xm_recv, f_send, f_recv, c_send, c_recv,
):
    dp, head = lax.axis_index("dp"), lax.axis_index("head")
    z, y = dp // YN, dp % YN
    x, core = head // CN, head % CN
    right = ((x + 1) % XN) * CN + core
    left = ((x + XN - 1) % XN) * CN + core
    across = ((x + 2) % XN) * CN + core
    twin = x * CN + 1 - core

    def peer(k):
        dz, dy = slot_offset(k)
        return ((z + dz) % ZN) * YN + (y + dy) % YN

    loads = [
        pltpu.make_async_copy(mem.at[:, 0:RM, pl.ds(pl.multiple_of(head * 256, 256), 256)], own, in_sem.at[0]),
        pltpu.make_async_copy(mem.at[:, RM:BLOCK, :], rest, in_sem.at[1]),
        pltpu.make_async_copy(wk, wts.at[:, 0:256], in_sem.at[2]),
        pltpu.make_async_copy(wv, wts.at[:, 256:512], in_sem.at[3]),
    ]
    for load in loads:
        load.start()

    barrier = pltpu.get_barrier_semaphore()

    def greet(k, _):
        pl.semaphore_signal(barrier, inc=1, device_id=(peer(k), head), device_id_type=MESH)
        return 0

    lax.fori_loop(1, NDP, greet, 0)
    for other in (right, left, twin):
        pl.semaphore_signal(barrier, inc=1, device_id=(dp, other), device_id_type=MESH)

    loads[0].wait()

    def fill(k, _):
        home = peer(k)
        packed[k] = own[table[0, home]]
        tag_out[k] = jnp.full((8, 128), table[1, home], jnp.int32)
        return 0

    lax.fori_loop(0, NDP, fill, 0)
    pool[head, pl.ds(0, RM), :] = packed[0]
    tags[0] = tag_out[0]
    pl.semaphore_wait(barrier, NDP - 1 + 3)

    def rows_of(k, count):
        return pl.ds(pl.multiple_of(k * RM, 16), count * RM)

    def a_copy(k):
        return pltpu.make_async_remote_copy(
            src_ref=packed.at[k], dst_ref=pool.at[head, rows_of(k, 1), :],
            send_sem=a_send.at[k], recv_sem=a_recv.at[k],
            device_id=(peer(k), head), device_id_type=MESH)

    def t_copy(k):
        return pltpu.make_async_remote_copy(
            src_ref=tag_out.at[k], dst_ref=tags.at[k],
            send_sem=t_send.at[k], recv_sem=t_recv.at[k],
            device_id=(peer(k), head), device_id_type=MESH)

    def d_copy(k):
        return pltpu.make_async_remote_copy(
            src_ref=kv_out.at[k], dst_ref=kv_dir.at[k],
            send_sem=d_send.at[k], recv_sem=d_recv.at[k],
            device_id=(peer(k), head), device_id_type=MESH)

    def each(first, last, act):
        def step(k, _):
            act(k)
            return 0

        lax.fori_loop(first, last, step, 0)

    each(1, NDP, lambda k: a_copy(k).start())

    loads[1].wait()
    loads[2].wait()
    loads[3].wait()
    slots = rest.shape[0]
    rest_rows = rest[...].reshape(slots * RK, rest.shape[2])
    rest_kv[...] = (
        jnp.dot(rest_rows, wts[...], preferred_element_type=jnp.float32)
        .astype(BF16)
        .reshape(slots, RK, 512)
    )

    def send_direct(k):
        kv_out[k] = rest_kv[table[0, peer(k)]]
        d_copy(k).start()
        t_copy(k).start()

    each(1, NDP, send_direct)
    kv_dir[0] = rest_kv[table[0, dp]]

    def head_copy(piece, group, target, send, recv):
        where = pool.at[piece, rows_of(group * GROUP, GROUP), :]
        return pltpu.make_async_remote_copy(
            src_ref=where, dst_ref=where, send_sem=send, recv_sem=recv,
            device_id=(dp, target), device_id_type=MESH)

    def plus_copy(g):
        return head_copy(head, g, right, xp_send.at[g], xp_recv.at[g])

    def minus_copy(g):
        return head_copy(head, g, left, xm_send.at[g], xm_recv.at[g])

    def forward_right(g):
        return head_copy(left, g, right, f_send.at[g], f_recv.at[g])

    def forward_left(g):
        return head_copy(right, g, left, f_send.at[g], f_recv.at[g])

    def core_copy(piece, n, g):
        return head_copy(piece, g, twin, c_send.at[n, g], c_recv.at[n, g])

    def stage_own(g):
        def arrived(k):
            pl.when(k > 0)(lambda: a_copy(k).wait_recv())

        each(g * GROUP, (g + 1) * GROUP, arrived)
        plus_copy(g).start()
        minus_copy(g).start()
        core_copy(head, 0, g).start()

    def stage_forward(g):
        plus_copy(g).wait_recv()
        minus_copy(g).wait_recv()
        pl.when(g % 2 == 0)(lambda: forward_right(g).start())
        pl.when(g % 2 == 1)(lambda: forward_left(g).start())
        core_copy(left, 1, g).start()
        core_copy(right, 2, g).start()

    def stage_core(g):
        forward_right(g).wait_recv()
        core_copy(across, 3, g).start()

    def stage_project(g):
        for n in range(4):
            core_copy(head, n, g).wait_recv()
        rows = rows_of(g * GROUP, GROUP)
        block = jnp.concatenate([pool[p, rows, :] for p in range(NHEAD)], axis=1)
        kv_mem[rows, :] = jnp.dot(block, wts[...], preferred_element_type=jnp.float32).astype(BF16)

    def round_of(t):
        for late, stage in enumerate((stage_own, stage_forward, stage_core, stage_project)):
            g = t - late * LAG
            pl.when((g >= 0) & (g < NGROUP))(functools.partial(stage, g))

    each(0, NGROUP + 3 * LAG, round_of)

    def settle(k):
        a_copy(k).wait_send()
        d_copy(k).wait()
        t_copy(k).wait()

    each(1, NDP, settle)

    def settle_group(g):
        plus_copy(g).wait_send()
        minus_copy(g).wait_send()
        forward_right(g).wait_send()
        for n in range(4):
            core_copy(head, n, g).wait_send()

    each(0, NGROUP, settle_group)


def move(table, memory, w_key, w_value):
    slots, depth = memory.shape[0], memory.shape[2]
    dma = pltpu.SemaphoreType.DMA
    vmem, smem, anywhere = (pl.BlockSpec(memory_space=s) for s in (pltpu.VMEM, pltpu.SMEM, pl.ANY))
    return pl.pallas_call(
        move_kernel,
        out_shape=(
            jax.ShapeDtypeStruct((NDP * RM, 512), BF16),
            jax.ShapeDtypeStruct((NDP, RK, 512), BF16),
            jax.ShapeDtypeStruct((NDP, 8, 128), jnp.int32),
        ),
        in_specs=[smem, anywhere, anywhere, anywhere],
        out_specs=(vmem, vmem, vmem),
        scratch_shapes=[
            pltpu.VMEM((slots, RM, 256), BF16),
            pltpu.VMEM((slots, RK, depth), BF16),
            pltpu.VMEM((slots, RK, 512), BF16),
            pltpu.VMEM((depth, 512), BF16),
            pltpu.VMEM((NDP, RM, 256), BF16),
            pltpu.VMEM((NDP, RK, 512), BF16),
            pltpu.VMEM((NDP, 8, 128), jnp.int32),
            pltpu.VMEM((NHEAD, NDP * RM, 256), BF16),
            dma((4,)),
            *[dma((NDP,)) for _ in range(6)],
            *[dma((NGROUP,)) for _ in range(6)],
            dma((4, NGROUP)),
            dma((4, NGROUP)),
        ],
        compiler_params=pltpu.CompilerParams(
            collective_id=0, has_side_effects=True, vmem_limit_bytes=56 * 2**20
        ),
        cost_estimate=pl.CostEstimate(
            flops=2 * NDP * BLOCK * depth * 512, bytes_accessed=24 * 2**20, transcendentals=0
        ),
        name="move",
    )(table, memory, w_key, w_value)


def attend_kernel(where_of, lengths, kv_mem, kv_dir, query, w_out, keys, values, partial, score, att, ctx):
    requests = query.shape[0]
    span = MAXB * BLOCK
    for r in range(requests):
        for b in range(MAXB):
            k = where_of[r * MAXB + b]
            used = lengths[r] > b * BLOCK
            high = kv_mem[pl.ds(pl.multiple_of(k * RM, 16), RM), :]
            low = kv_dir[k]
            high = jnp.where(used, high, jnp.zeros_like(high))
            low = jnp.where(used, low, jnp.zeros_like(low))
            keys[r, b * BLOCK : b * BLOCK + RM, :] = high[:, 0:256]
            keys[r, b * BLOCK + RM : (b + 1) * BLOCK, :] = low[:, 0:256]
            values[r, b * BLOCK : b * BLOCK + RM, :] = high[:, 256:512]
            values[r, b * BLOCK + RM : (b + 1) * BLOCK, :] = low[:, 256:512]
    own_head = lax.broadcasted_iota(jnp.int32, (8, 256), 1) // HEAD_DIM == lax.broadcasted_iota(
        jnp.int32, (8, 256), 0
    )
    for r in range(requests):
        spread = jnp.where(own_head, jnp.broadcast_to(query[r : r + 1, :].astype(jnp.float32), (8, 256)), 0.0)
        dots = lax.dot_general(
            spread.astype(BF16), keys[r], (((1,), (1,)), ((), ())), preferred_element_type=jnp.float32
        )
        position = lax.broadcasted_iota(jnp.int32, (8, span), 1)
        score[r * 8 : (r + 1) * 8, :] = jnp.where(position < lengths[r], dots, -1e30)
    scores = score[...]
    expo = jnp.exp(scores - jnp.max(scores, axis=1, keepdims=True))
    att[...] = (expo / jnp.sum(expo, axis=1, keepdims=True)).astype(BF16)
    ctx[...] = jnp.zeros_like(ctx)
    for r in range(requests):
        mixed = jnp.dot(att[r * 8 : (r + 1) * 8, :], values[r], preferred_element_type=jnp.float32)
        ctx[r : r + 1, :] = jnp.sum(jnp.where(own_head, mixed, 0.0), axis=0, keepdims=True)
    summed = jnp.dot(ctx[...].astype(BF16), w_out[...], preferred_element_type=jnp.float32)
    for p in range(NHEAD):
        partial[p] = summed[:, p * 256 : (p + 1) * 256]


def attend(where_of, lengths, kv_mem, kv_dir, query, w_out):
    requests = query.shape[0]
    span = MAXB * BLOCK
    vmem, smem = (pl.BlockSpec(memory_space=s) for s in (pltpu.VMEM, pltpu.SMEM))
    return pl.pallas_call(
        attend_kernel,
        out_shape=(
            jax.ShapeDtypeStruct((requests, span, 256), BF16),
            jax.ShapeDtypeStruct((requests, span, 256), BF16),
            jax.ShapeDtypeStruct((NHEAD, 8, 256), jnp.float32),
        ),
        in_specs=[smem, smem, vmem, vmem, vmem, vmem],
        out_specs=(vmem, vmem, vmem),
        scratch_shapes=[
            pltpu.VMEM((requests * 8, span), jnp.float32),
            pltpu.VMEM((requests * 8, span), BF16),
            pltpu.VMEM((8, 256), jnp.float32),
        ],
        compiler_params=pltpu.CompilerParams(vmem_limit_bytes=40 * 2**20),
        name="attend",
    )(where_of, lengths, kv_mem, kv_dir, query, w_out)


def sum_kernel(partial, hidden, out, parts, send, recv):
    dp, head = lax.axis_index("dp"), lax.axis_index("head")
    barrier = pltpu.get_barrier_semaphore()
    for step in range(1, NHEAD):
        other = (head + step) % NHEAD
        pl.semaphore_signal(barrier, inc=1, device_id=(dp, other), device_id_type=MESH)
    pl.semaphore_wait(barrier, NHEAD - 1)
    copies = []
    for step in range(1, NHEAD):
        other = (head + step) % NHEAD
        copy = pltpu.make_async_remote_copy(
            src_ref=partial.at[other], dst_ref=parts.at[step], send_sem=send.at[step], recv_sem=recv.at[step],
            device_id=(dp, other), device_id_type=MESH)
        copy.start()
        copies.append(copy)
    total = partial[head]
    for step, copy in enumerate(copies, 1):
        copy.wait_recv()
        total = total + parts[step]
    requests = hidden.shape[0]
    out[...] = (hidden[...].astype(jnp.float32) + total[0:requests, :]).astype(BF16)
    for copy in copies:
        copy.wait_send()


def sum_heads(partial, hidden):
    vmem = pl.BlockSpec(memory_space=pltpu.VMEM)
    return pl.pallas_call(
        sum_kernel,
        out_shape=jax.ShapeDtypeStruct(hidden.shape, BF16),
        in_specs=[vmem, vmem],
        out_specs=vmem,
        scratch_shapes=[
            pltpu.VMEM((NHEAD, 8, 256), jnp.float32),
            pltpu.SemaphoreType.DMA((NHEAD,)),
            pltpu.SemaphoreType.DMA((NHEAD,)),
        ],
        compiler_params=pltpu.CompilerParams(collective_id=1, has_side_effects=True),
        name="sum_heads",
    )(partial, hidden)


def shards(memory, block_route, enc_len, w_key, w_value, dec_query, dec_hidden, w_out):
    slots = block_route.shape[1]
    cells = enc_len.shape[0] * MAXB
    to_home = block_route[0][None, :] == jnp.arange(NDP)[:, None]
    index = jnp.sum(jnp.where(to_home, jnp.arange(slots)[None, :], 0), axis=1)
    cell = jnp.sum(jnp.where(to_home, block_route[1][None, :] + 1, 0), axis=1) - 1
    table = jnp.stack([index, cell]).astype(jnp.int32)
    blocks = memory.reshape(slots, BLOCK, memory.shape[1])
    kv_mem, kv_dir, tags = move(table, blocks, w_key, w_value)
    from_slot = tags[:, 0, 0][None, :] == jnp.arange(cells)[:, None]
    where_of = jnp.sum(jnp.where(from_slot, jnp.arange(NDP)[None, :], 0), axis=1).astype(jnp.int32)
    keys, values, partial = attend(where_of, enc_len, kv_mem, kv_dir, dec_query, w_out)
    new_hidden = sum_heads(partial, dec_hidden)
    return new_hidden, keys, values


def solution(mesh):
    in_specs = (
        P("dp", None),
        P(None, "dp"),
        P("dp"),
        P(None, "head"),
        P(None, "head"),
        P("dp", "head"),
        P("dp", "head"),
        P("head", None),
    )
    out_specs = (P("dp", "head"), P("dp", None, "head"), P("dp", None, "head"))
    return jax.shard_map(shards, mesh=mesh, in_specs=in_specs, out_specs=out_specs, check_vma=False)
```

time: 586 us -> 114 us (0.19)
  waiting for transfers between devices: 429 us -> 0 us
  Pallas kernels: 0 us -> 105 us
  local copies, waits for them, and re-layouts: 97.1 us -> 6.55 us
  starting transfers between devices: 21.6 us -> 0 us
  matrix products: 19.2 us -> 0 us
  between operations: 14.1 us -> 0.69 us
    all_to_all x2 -> x0, waiting for transfers between devices: 372 us -> none  [the longest x1 372 us: shards(): lax.all_to_all(buffer, 'dp', split_axis=0, concat_axis=0, tiled=True)]
    pallas_call x0 -> x3, Pallas kernels: none -> 105 us  [the longest x1 93.4 us: move(): pl.pallas_call(move_kernel, out_shape=(jax.ShapeDtypeStruct((NDP * RM, 51...]
    scatter x3 -> x0, local copies, waits for them, and re-layouts: 63.4 us -> none  [the longest x1 41.8 us: shards(): home_grid = jnp.zeros((grid_size + 1, BLOCK, columns), memory_buffer.dtyp...]
    reduce_scatter x1 -> x0, waiting for transfers between devices: 56.9 us -> none  [shards(): lax.psum_scatter(partial_out, 'head', scatter_dimension=1, tiled=True)]
    all_to_all x2 -> x0, starting transfers between devices: 21.6 us -> none  [the longest x1 12 us: shards(): lax.all_to_all(block_tags, 'dp', split_axis=0, concat_axis=0, tiled=True)]
    dot_general x5 -> x0, matrix products: 19.2 us -> none  [the longest x1 9.39 us: shards(): jnp.dot(flat_rows, w_value, preferred_element_type=jnp.float32)]
    broadcast_in_dim x2 -> x0, local copies, waits for them, and re-layouts: 12.3 us -> none  [the longest x1 6.33 us: shards(): jnp.zeros((grid_size + 1, BLOCK, columns), memory_buffer.dtype)]
    reshape x4 -> x0, local copies, waits for them, and re-layouts: 8.94 us -> none  [the longest x1 5.78 us: shards(): value_grid = value_flat.reshape(req_count, span, local_heads, HEAD_DIM)]
  transfers between devices with their start and end apart: 3 -> 0, of which waited for: 2 -> 0; matrix products, arithmetic and copies ran while one was open for 5% -> 0% of each run, Pallas kernels for 0% -> 0%
where the time goes in v1:
time: 114 us
  Pallas kernels  105 us (92%)
  local copies, waits for them, and re-layouts  6.55 us (6%)
  other arithmetic  1.54 us (1%)
    pallas_call x1, Pallas kernels, move(): pl.pallas_call(move_kernel, out_shape=(jax.ShapeDtypeStruct((NDP * RM, 51...  93.4 us
    pallas_call x1, Pallas kernels, sum_heads(): pl.pallas_call(sum_kernel, out_shape=jax.ShapeDtypeStruct(hidden.shape, B...  9.11 us
    unnamed x13, local copies, waits for them, and re-layouts  4.97 us
    pallas_call x1, Pallas kernels, attend(): pl.pallas_call(attend_kernel, out_shape=(jax.ShapeDtypeStruct((requests,...  2.82 us

profile of v1, /device:TPU:1, one launch (start us, length us, event | category | flops | bytes accessed | tf_op | source)
XLA Modules:
  0.0 114.1 jit_solution(15147585565982043110)
XLA Ops:
  0.6 0.8 add_bitcast_fusion.1
  1.4 0.1 select_reduce_fusion.2
  1.5 0.6 pad_add_fusion.table
  2.1 0.0 copy-start.1
  2.1 0.0 copy-start.4
  2.1 0.0 copy-start.5
  2.1 93.4 %move.1 = (bf16[3584,512]{1,0:T(8,128)(2,1)}, bf16[32,16,512]{2,1,0:T(8,128)(2,1)}, s32[32,8,128]{2,1,0:T(8,128)}) custom-call(s32[2,32]{1,0:T(2,128)} %pad_add_fusion.table, bf16[15,128,2048]{2,1,0:T(8,128)(2,1)} %bitcast.9, bf16[2048,256]{1,0:T(8,128)(2,1)} %wk.1, bf16[2048,256]{1,0:T(8,128)(2,1)} %wv.1), custom_call_target="tpu_custom_call" | custom-call | flops 8589934592 | bytes 25165824 | tf_op jit(solution)/shard_map/move/pallas_call | solution.py:207
  95.5 1.6 %slice_reduce_fusion = s32[32]{0:T(128)S(1)} fusion(s32[32,8,128]{2,1,0:T(8,128)} %get-tuple-element.9), kind=kLoop, calls=%fused_computation | loop fusion | bytes 256 | tf_op jit(solution)/shard_map/slice | solution.py:352
  97.0 0.1 select_reduce_fusion.where_of
  97.2 0.0 copy-done.1
  97.2 0.0 copy-done.4
  97.2 0.0 copy-done.5
  97.2 0.0 copy-start
  97.2 2.0 %copy-done = bf16[3584,512]{1,0:T(8,128)(2,1)S(1)} copy-done((bf16[3584,512]{1,0:T(8,128)(2,1)S(1)}, bf16[3584,512]{1,0:T(8,128)(2,1)}, u32[]{:S(2)}) %copy-start) | copy-done | bytes 3670040
  99.2 0.0 copy-start.2
  99.2 1.0 copy-done.2
  100.3 2.8 %attend.1 = (bf16[6,512,256]{2,1,0:T(8,128)(2,1)}, bf16[6,512,256]{2,1,0:T(8,128)(2,1)}, f32[8,8,256]{2,1,0:T(8,128)S(1)}) custom-call(s32[24]{0:T(128)S(1)} %select_reduce_fusion.where_of, s32[6]{0:T(128)S(1)} %copy-done.5, bf16[3584,512]{1,0:T(8,128)(2,1)S(1)} %copy-done, bf16[32,16,512]{2,1,0:T(8,128)(2,1)S(1)} %copy-done.2, ...), custom_call_target="tpu_custom_call" | custom-call | tf_op jit(solution)/shard_map/attend/pallas_call | solution.py:282
  103.1 0.0 copy-start.3
  103.1 0.6 copy-done.3
  103.7 9.1 %sum_heads.1 = bf16[6,256]{1,0:T(8,128)(2,1)} custom-call(f32[8,8,256]{2,1,0:T(8,128)} %copy-done.3, bf16[6,256]{1,0:T(8,128)(2,1)} %hidden.1), custom_call_target="tpu_custom_call" | custom-call | tf_op jit(solution)/shard_map/sum_heads/pallas_call | solution.py:328
  112.8 1.3 %copy.12 = bf16[6,256]{1,0:T(8,128)(2,1)} copy(bf16[6,256]{1,0:T(8,128)(2,1)} %sum_heads.1) | data formatting | bytes 6144
  (1 shorter events, 0.0 us)
Async XLA Ops:
  2.1 95.1 %copy-start.1 = (bf16[256,2048]{1,0:T(8,128)(2,1)S(1)}, bf16[256,2048]{1,0:T(8,128)(2,1)}, u32[]{:S(2)}) copy-start(bf16[256,2048]{1,0:T(8,128)(2,1)} %w_out.1) | copy-start | bytes 3145732
  2.1 95.1 %copy-start.4 = (bf16[6,256]{1,0:T(8,128)(2,1)S(1)}, bf16[6,256]{1,0:T(8,128)(2,1)}, u32[]{:S(2)}) copy-start(bf16[6,256]{1,0:T(8,128)(2,1)} %query.1) | copy-start | bytes 9220
  2.1 95.1 %copy-start.5 = (s32[6]{0:T(128)S(1)}, s32[6]{0:T(128)}, u32[]{:S(2)}) copy-start(s32[6]{0:T(128)} %lengths.1) | copy-start | bytes 76
  97.2 2.0 %copy-start = (bf16[3584,512]{1,0:T(8,128)(2,1)S(1)}, bf16[3584,512]{1,0:T(8,128)(2,1)}, u32[]{:S(2)}) copy-start(bf16[3584,512]{1,0:T(8,128)(2,1)} %get-tuple-element.10.kv_mem) | copy-start | bytes 11010052
  99.2 1.0 copy-start.2
  103.1 0.6 copy-start.3

commit v2 on v0

v2 whole, which is shorter than its diff:
```python
import functools

import jax
import jax.numpy as jnp
from jax import lax
from jax.experimental import pallas as pl
from jax.experimental.pallas import tpu as pltpu
from jax.sharding import PartitionSpec as P

HEAD_DIM = 64
BLOCK = 128
MAXB = 4
ZN, YN, XN, CN = 8, 4, 4, 2
NDP, NHEAD = ZN * YN, XN * CN
COLS = 256
DIRECT = 10
GROUP = 2
LAG = 1
NMEM = NDP - DIRECT
NGROUP = NMEM // GROUP
MESH = pl.DeviceIdType.MESH
BF16 = jnp.bfloat16
F32 = jnp.float32


def slot_offset(k):
    outer = (k + NDP - YN) // NDP
    last = k // (NDP - YN)
    middle = outer - last
    m = (k + NDP - YN) % NDP
    dz = middle * (m // 8 + 1) * (1 - 2 * (m % 2)) + last * (ZN // 2) + ZN
    j = (1 - outer) * k + middle * ((m % 8) // 2) + last * (k - NDP + YN)
    dy = (j % 2) * ((j + 1) // 2) + (1 - j % 2) * (YN - j // 2)
    return dz, dy


def each(first, last, act):
    def step(k, _):
        act(k)
        return 0

    lax.fori_loop(first, last, step, 0)


def whole_kernel(
    route, lengths, query, hidden, mem, wk, wv, wo, new_hidden, keys, values,
    own, full, wts, wout, packed, kv_out, tag_out, tags, place, pool, kv, key_grid, value_grid,
    score, att, ctx, partial, parts, home_of, cells,
    in_sem, a_send, a_recv, d_send, d_recv, t_send, t_recv,
    xp_send, xp_recv, xm_send, xm_recv, f_send, f_recv, c_send, c_recv, s_send, s_recv, out_sem,
):
    dp, head = lax.axis_index("dp"), lax.axis_index("head")
    z, y = dp // YN, dp % YN
    x, core = head // CN, head % CN
    right = ((x + 1) % XN) * CN + core
    left = ((x + XN - 1) % XN) * CN + core
    across = ((x + 2) % XN) * CN + core
    twin = x * CN + 1 - core
    slots = mem.shape[0]
    requests = query.shape[0]

    def peer(k):
        dz, dy = slot_offset(k)
        return ((z + dz) % ZN) * YN + (y + dy) % YN

    columns = pl.ds(pl.multiple_of(head * COLS, COLS), COLS)
    loads = [
        pltpu.make_async_copy(mem.at[:, :, columns], own, in_sem.at[0]),
        pltpu.make_async_copy(mem, full, in_sem.at[1]),
        pltpu.make_async_copy(wk, wts.at[:, 0:COLS], in_sem.at[2]),
        pltpu.make_async_copy(wv, wts.at[:, COLS : 2 * COLS], in_sem.at[3]),
        pltpu.make_async_copy(wo, wout, in_sem.at[4]),
    ]
    for load in loads:
        load.start()

    barrier = pltpu.get_barrier_semaphore()

    def greet(k):
        pl.semaphore_signal(barrier, inc=1, device_id=(peer(k), head), device_id_type=MESH)

    each(1, NDP, greet)
    for step in range(1, NHEAD):
        pl.semaphore_signal(barrier, inc=1, device_id=(dp, (head + step) % NHEAD), device_id_type=MESH)

    to_home = [route[0, j] for j in range(slots)]

    def look_up(k):
        home = peer(k)
        index, cell = jnp.int32(0), jnp.int32(-1)
        for j in range(slots):
            hit = to_home[j] == home
            index = jnp.where(hit, j, index)
            cell = jnp.where(hit, route[1, j], cell)
        home_of[k] = index
        tag_out[k] = jnp.full((1, 128), cell, jnp.int32)

    each(0, NDP, look_up)
    tags[0] = tag_out[0]

    loads[0].wait()

    def fill(k):
        packed[k - DIRECT] = own[home_of[k]]

    each(DIRECT, NDP, fill)
    pl.semaphore_wait(barrier, NDP - 1 + NHEAD - 1)

    def rows_of(g):
        return pl.ds(pl.multiple_of(g * (GROUP * BLOCK), GROUP * BLOCK), GROUP * BLOCK)

    def a_copy(k):
        rows = pl.ds(pl.multiple_of((k - DIRECT) * BLOCK, BLOCK), BLOCK)
        return pltpu.make_async_remote_copy(
            src_ref=packed.at[k - DIRECT], dst_ref=pool.at[head, rows, :],
            send_sem=a_send.at[k], recv_sem=a_recv.at[k],
            device_id=(peer(k), head), device_id_type=MESH)

    def t_copy(k):
        return pltpu.make_async_remote_copy(
            src_ref=tag_out.at[k], dst_ref=tags.at[k],
            send_sem=t_send.at[k], recv_sem=t_recv.at[k],
            device_id=(peer(k), head), device_id_type=MESH)

    def d_copy(k):
        return pltpu.make_async_remote_copy(
            src_ref=kv_out.at[k], dst_ref=kv.at[k],
            send_sem=d_send.at[k], recv_sem=d_recv.at[k],
            device_id=(peer(k), head), device_id_type=MESH)

    each(DIRECT, NDP, lambda k: a_copy(k).start())

    def project(rows):
        return jnp.dot(rows, wts[...], preferred_element_type=F32).astype(BF16)

    for load in loads[1:4]:
        load.wait()

    def direct_group(g):
        base = g * GROUP
        rows = jnp.concatenate([full[home_of[base + i]] for i in range(GROUP)], axis=0)
        kv_out[pl.ds(base, GROUP)] = project(rows).reshape(GROUP, BLOCK, 2 * COLS)
        for i in range(GROUP):
            pl.when(base + i > 0)(lambda k=base + i: d_copy(k).start())

    each(0, DIRECT // GROUP, direct_group)
    kv[0] = kv_out[0]
    each(1, NDP, lambda k: t_copy(k).start())

    def head_copy(piece, group, target, send, recv):
        where = pool.at[piece, rows_of(group), :]
        return pltpu.make_async_remote_copy(
            src_ref=where, dst_ref=where, send_sem=send, recv_sem=recv,
            device_id=(dp, target), device_id_type=MESH)

    def plus_copy(g):
        return head_copy(head, g, right, xp_send.at[g], xp_recv.at[g])

    def minus_copy(g):
        return head_copy(head, g, left, xm_send.at[g], xm_recv.at[g])

    def forward_right(g):
        return head_copy(left, g, right, f_send.at[g], f_recv.at[g])

    def forward_left(g):
        return head_copy(right, g, left, f_send.at[g], f_recv.at[g])

    def core_copy(piece, n, g):
        return head_copy(piece, g, twin, c_send.at[n, g], c_recv.at[n, g])

    def stage_own(g):
        each(DIRECT + g * GROUP, DIRECT + (g + 1) * GROUP, lambda k: a_copy(k).wait_recv())
        plus_copy(g).start()
        minus_copy(g).start()
        core_copy(head, 0, g).start()

    def stage_forward(g):
        plus_copy(g).wait_recv()
        minus_copy(g).wait_recv()
        pl.when(g % 2 == 0)(lambda: forward_right(g).start())
        pl.when(g % 2 == 1)(lambda: forward_left(g).start())
        core_copy(left, 1, g).start()
        core_copy(right, 2, g).start()

    def stage_core(g):
        forward_right(g).wait_recv()
        core_copy(across, 3, g).start()

    def stage_project(g):
        for n in range(4):
            core_copy(head, n, g).wait_recv()
        rows = jnp.concatenate([pool[p, rows_of(g), :] for p in range(NHEAD)], axis=1)
        kv[pl.ds(DIRECT + g * GROUP, GROUP)] = project(rows).reshape(GROUP, BLOCK, 2 * COLS)

    def round_of(t):
        for late, stage in enumerate((stage_own, stage_forward, stage_core, stage_project)):
            g = t - late * LAG
            pl.when((g >= 0) & (g < NGROUP))(functools.partial(stage, g))

    each(0, NGROUP + 2 * LAG, round_of)

    each(1, NDP, lambda k: t_copy(k).wait_recv())
    lane = lax.broadcasted_iota(jnp.int32, (NDP, 1, 128), 2)
    slot = lax.broadcasted_iota(jnp.int32, (NDP, 1, 128), 0)
    place[...] = jnp.max(jnp.where(tags[...] == lane, slot, 0), axis=0)
    to_scalars = pltpu.make_async_copy(place, cells, in_sem.at[5])
    to_scalars.start()

    each(NGROUP + 2 * LAG, NGROUP + 3 * LAG, round_of)
    each(1, DIRECT, lambda k: d_copy(k).wait_recv())
    to_scalars.wait()

    span = MAXB * BLOCK
    outs = []
    for r in range(requests):
        for b in range(MAXB):
            block = kv[cells[0, r * MAXB + b]]
            block = jnp.where(lengths[r] > b * BLOCK, block, jnp.zeros_like(block))
            key_grid[r, b * BLOCK : (b + 1) * BLOCK, :] = block[:, 0:COLS]
            value_grid[r, b * BLOCK : (b + 1) * BLOCK, :] = block[:, COLS : 2 * COLS]
        outs.append(pltpu.make_async_copy(key_grid.at[r], keys.at[r], out_sem.at[0, r]))
        outs.append(pltpu.make_async_copy(value_grid.at[r], values.at[r], out_sem.at[1, r]))
        for copy in outs[-2:]:
            copy.start()

    own_head = lax.broadcasted_iota(jnp.int32, (8, COLS), 1) // HEAD_DIM == lax.broadcasted_iota(
        jnp.int32, (8, COLS), 0
    )
    position = lax.broadcasted_iota(jnp.int32, (8, span), 1)
    for r in range(requests):
        spread = jnp.where(own_head, jnp.broadcast_to(query[r : r + 1, :].astype(F32), (8, COLS)), 0.0)
        dots = lax.dot_general(
            spread.astype(BF16), key_grid[r], (((1,), (1,)), ((), ())), preferred_element_type=F32
        )
        score[r * 8 : (r + 1) * 8, :] = jnp.where(position < lengths[r], dots, -1e30)
    scores = score[...]
    expo = jnp.exp(scores - jnp.max(scores, axis=1, keepdims=True))
    att[...] = (expo / jnp.sum(expo, axis=1, keepdims=True)).astype(BF16)
    ctx[...] = jnp.zeros_like(ctx)
    for r in range(requests):
        mixed = jnp.dot(att[r * 8 : (r + 1) * 8, :], value_grid[r], preferred_element_type=F32)
        ctx[r : r + 1, :] = jnp.sum(jnp.where(own_head, mixed, 0.0), axis=0, keepdims=True)
    loads[4].wait()
    summed = jnp.dot(ctx[...].astype(BF16), wout[...], preferred_element_type=F32)
    for p in range(NHEAD):
        partial[p] = summed[:, p * COLS : (p + 1) * COLS]

    def s_copy(step):
        other = (head + step) % NHEAD
        return pltpu.make_async_remote_copy(
            src_ref=partial.at[other], dst_ref=parts.at[step],
            send_sem=s_send.at[step], recv_sem=s_recv.at[step],
            device_id=(dp, other), device_id_type=MESH)

    for step in range(1, NHEAD):
        s_copy(step).start()

    each(DIRECT, NDP, lambda k: a_copy(k).wait_send())
    each(1, DIRECT, lambda k: d_copy(k).wait_send())
    each(1, NDP, lambda k: t_copy(k).wait_send())

    def settle_group(g):
        plus_copy(g).wait_send()
        minus_copy(g).wait_send()
        forward_right(g).wait_send()
        for n in range(4):
            core_copy(head, n, g).wait_send()

    each(0, NGROUP, settle_group)

    total = partial[head]
    for step in range(1, NHEAD):
        s_copy(step).wait_recv()
        total = total + parts[step]
    new_hidden[...] = (hidden[...].astype(F32) + total[0:requests, :]).astype(BF16)
    for step in range(1, NHEAD):
        s_copy(step).wait_send()
    for copy in outs:
        copy.wait()


def shards(memory, block_route, enc_len, w_key, w_value, dec_query, dec_hidden, w_out):
    slots, depth, requests = block_route.shape[1], memory.shape[1], enc_len.shape[0]
    span = MAXB * BLOCK
    dma, bufs = pltpu.SemaphoreType.DMA, pltpu.VMEM
    vmem, smem, anywhere = (pl.BlockSpec(memory_space=s) for s in (pltpu.VMEM, pltpu.SMEM, pl.ANY))
    grid = jax.ShapeDtypeStruct((requests, span, COLS), BF16)
    return pl.pallas_call(
        whole_kernel,
        out_shape=(jax.ShapeDtypeStruct(dec_hidden.shape, BF16), grid, grid),
        in_specs=[smem, smem, vmem, vmem, anywhere, anywhere, anywhere, anywhere],
        out_specs=(vmem, anywhere, anywhere),
        scratch_shapes=[
            bufs((slots, BLOCK, COLS), BF16),
            bufs((slots, BLOCK, depth), BF16),
            bufs((depth, 2 * COLS), BF16),
            bufs((COLS, depth), BF16),
            bufs((NMEM, BLOCK, COLS), BF16),
            bufs((DIRECT, BLOCK, 2 * COLS), BF16),
            bufs((NDP, 1, 128), jnp.int32),
            bufs((NDP, 1, 128), jnp.int32),
            bufs((1, 128), jnp.int32),
            bufs((NHEAD, NMEM * BLOCK, COLS), BF16),
            bufs((NDP, BLOCK, 2 * COLS), BF16),
            bufs((requests, span, COLS), BF16),
            bufs((requests, span, COLS), BF16),
            bufs((requests * 8, span), F32),
            bufs((requests * 8, span), BF16),
            bufs((8, COLS), F32),
            bufs((NHEAD, 8, COLS), F32),
            bufs((NHEAD, 8, COLS), F32),
            pltpu.SMEM((NDP,), jnp.int32),
            pltpu.SMEM((1, 128), jnp.int32),
            dma((6,)),
            *[dma((NDP,)) for _ in range(6)],
            *[dma((NGROUP,)) for _ in range(6)],
            dma((4, NGROUP)),
            dma((4, NGROUP)),
            dma((NHEAD,)),
            dma((NHEAD,)),
            dma((2, requests)),
        ],
        compiler_params=pltpu.CompilerParams(
            collective_id=0, has_side_effects=True, vmem_limit_bytes=56 * 2**20
        ),
        cost_estimate=pl.CostEstimate(
            flops=2 * NDP * BLOCK * depth * 2 * COLS, bytes_accessed=24 * 2**20, transcendentals=0
        ),
        name="whole",
    )(block_route, enc_len, dec_query, dec_hidden, memory.reshape(slots, BLOCK, depth), w_key, w_value, w_out)


def solution(mesh):
    in_specs = (
        P("dp", None),
        P(None, "dp"),
        P("dp"),
        P(None, "head"),
        P(None, "head"),
        P("dp", "head"),
        P("dp", "head"),
        P("head", None),
    )
    out_specs = (P("dp", "head"), P("dp", None, "head"), P("dp", None, "head"))
    return jax.shard_map(shards, mesh=mesh, in_specs=in_specs, out_specs=out_specs, check_vma=False)
```

time: 586 us -> 88.8 us (0.15)
  waiting for transfers between devices: 429 us -> 0 us
  local copies, waits for them, and re-layouts: 97.1 us -> 5.19 us
  Pallas kernels: 0 us -> 82 us
  starting transfers between devices: 21.6 us -> 0 us
  matrix products: 19.2 us -> 0 us
  between operations: 14.1 us -> 0.64 us
    all_to_all x2 -> x0, waiting for transfers between devices: 372 us -> none  [the longest x1 372 us: shards(): lax.all_to_all(buffer, 'dp', split_axis=0, concat_axis=0, tiled=True)]
    pallas_call x0 -> x1, Pallas kernels: none -> 82 us  [shards(): pl.pallas_call(whole_kernel, out_shape=(jax.ShapeDtypeStruct(dec_hidden.s...]
    scatter x3 -> x0, local copies, waits for them, and re-layouts: 63.4 us -> none  [the longest x1 41.8 us: shards(): home_grid = jnp.zeros((grid_size + 1, BLOCK, columns), memory_buffer.dtyp...]
    reduce_scatter x1 -> x0, waiting for transfers between devices: 56.9 us -> none  [shards(): lax.psum_scatter(partial_out, 'head', scatter_dimension=1, tiled=True)]
    all_to_all x2 -> x0, starting transfers between devices: 21.6 us -> none  [the longest x1 12 us: shards(): lax.all_to_all(block_tags, 'dp', split_axis=0, concat_axis=0, tiled=True)]
    dot_general x5 -> x0, matrix products: 19.2 us -> none  [the longest x1 9.39 us: shards(): jnp.dot(flat_rows, w_value, preferred_element_type=jnp.float32)]
    broadcast_in_dim x2 -> x0, local copies, waits for them, and re-layouts: 12.3 us -> none  [the longest x1 6.33 us: shards(): jnp.zeros((grid_size + 1, BLOCK, columns), memory_buffer.dtype)]
    reshape x4 -> x0, local copies, waits for them, and re-layouts: 8.94 us -> none  [the longest x1 5.78 us: shards(): value_grid = value_flat.reshape(req_count, span, local_heads, HEAD_DIM)]
  transfers between devices with their start and end apart: 3 -> 0, of which waited for: 2 -> 0; matrix products, arithmetic and copies ran while one was open for 5% -> 0% of each run, Pallas kernels for 0% -> 0%
where the time goes in v2:
time: 88.8 us; the launch traced here: 87.8 us
  Pallas kernels  82 us (92%)
  local copies, waits for them, and re-layouts  5.19 us (6%)
    pallas_call x1, Pallas kernels, shards(): pl.pallas_call(whole_kernel, out_shape=(jax.ShapeDtypeStruct(dec_hidden.s...  82 us
    unnamed x5, local copies, waits for them, and re-layouts  5.19 us

profile of v2, /device:TPU:1, one launch (start us, length us, event | category | flops | bytes accessed | tf_op | source)
XLA Modules:
  0.0 87.8 jit_solution(14120945470207213028)
XLA Ops:
  0.6 82.0 %whole.1 = (bf16[6,256]{1,0:T(8,128)(2,1)}, bf16[6,512,256]{2,1,0:T(8,128)(2,1)}, bf16[6,512,256]{2,1,0:T(8,128)(2,1)}) custom-call(s32[2,15]{1,0:T(2,128)} %route.1, s32[6]{0:T(128)} %lengths.1, bf16[6,256]{1,0:T(8,128)(2,1)} %query.1, bf16[6,256]{1,0:T(8,128)(2,1)} %hidden.1, bf16[15,128,2048]{2,1,0:T(8,128)(2,1)} %bitcast.1, bf16[2048,256]{1,0:T(8,128)(2,1)} %wk.1, ...), custom_call_target="tpu_custom_call" | custom-call | flops 8589934592 | bytes 25165824 | tf_op jit(solution)/shard_map/whole/pallas_call | solution.py:288
  82.6 1.3 %copy.14 = bf16[6,256]{1,0:T(8,128)(2,1)} copy(bf16[6,256]{1,0:T(8,128)(2,1)} %get-tuple-element.6) | data formatting | bytes 6144
  83.9 0.0 copy-start
  83.9 2.8 %copy.15 = bf16[6,512,256]{2,1,0:T(8,128)(2,1)} copy(bf16[6,512,256]{2,1,0:T(8,128)(2,1)} %get-tuple-element.7) | data formatting | bytes 3145728
  86.7 0.0 copy-done
  86.7 1.1 %copy.16 = bf16[6,512,256]{2,1,0:T(8,128)(2,1)} copy(bf16[6,512,256]{2,1,0:T(8,128)(2,1)S(1)} %copy-done) | data formatting | bytes 3145728
Async XLA Ops:
  83.9 2.8 %copy-start = (bf16[6,512,256]{2,1,0:T(8,128)(2,1)S(1)}, bf16[6,512,256]{2,1,0:T(8,128)(2,1)}, u32[]{:S(2)}) copy-start(bf16[6,512,256]{2,1,0:T(8,128)(2,1)} %get-tuple-element.8) | copy-start | bytes 4718596

commit v3 on v2

--- a/solution.py
+++ b/solution.py
@@ -16,6 +16,8 @@
 DIRECT = 10
 GROUP = 2
 LAG = 1
+
+EARLY = 3
 NMEM = NDP - DIRECT
 NGROUP = NMEM // GROUP
 MESH = pl.DeviceIdType.MESH
@@ -30,7 +32,8 @@
     m = (k + NDP - YN) % NDP
     dz = middle * (m // 8 + 1) * (1 - 2 * (m % 2)) + last * (ZN // 2) + ZN
     j = (1 - outer) * k + middle * ((m % 8) // 2) + last * (k - NDP + YN)
-    dy = (j % 2) * ((j + 1) // 2) + (1 - j % 2) * (YN - j // 2)
+    turn = 1 - 2 * middle * (m % 2)
+    dy = turn * ((j % 2) * ((j + 1) // 2) - (1 - j % 2) * (j // 2)) + YN
     return dz, dy
 
 
@@ -43,67 +46,63 @@
 
 
 def whole_kernel(
-    route, lengths, query, hidden, mem, wk, wv, wo, new_hidden, keys, values,
+    route_in, lengths_in, query_in, hidden_in, mem, wk, wv, wo, new_hidden, keys, values,
     own, full, wts, wout, packed, kv_out, tag_out, tags, place, pool, kv, key_grid, value_grid,
-    score, att, ctx, partial, parts, home_of, cells,
+    score, att, ctx, partial, parts, home_of, cells, route, lengths, query, hidden, summed_hidden,
     in_sem, a_send, a_recv, d_send, d_recv, t_send, t_recv,
     xp_send, xp_recv, xm_send, xm_recv, f_send, f_recv, c_send, c_recv, s_send, s_recv, out_sem,
 ):
     dp, head = lax.axis_index("dp"), lax.axis_index("head")
-    z, y = dp // YN, dp % YN
-    x, core = head // CN, head % CN
-    right = ((x + 1) % XN) * CN + core
-    left = ((x + XN - 1) % XN) * CN + core
-    across = ((x + 2) % XN) * CN + core
+    z, y = lax.div(dp, YN), lax.rem(dp, YN)
+    x, core = lax.div(head, CN), lax.rem(head, CN)
+    right = lax.rem(x + 1, XN) * CN + core
+    left = lax.rem(x + XN - 1, XN) * CN + core
+    across = lax.rem(x + 2, XN) * CN + core
     twin = x * CN + 1 - core
     slots = mem.shape[0]
-    requests = query.shape[0]
+    requests = keys.shape[0]
 
     def peer(k):
         dz, dy = slot_offset(k)
-        return ((z + dz) % ZN) * YN + (y + dy) % YN
+        return lax.rem(z + dz, ZN) * YN + lax.rem(y + dy, YN)
 
     columns = pl.ds(pl.multiple_of(head * COLS, COLS), COLS)
+    get_route = pltpu.make_async_copy(route_in, route, in_sem.at[6])
+    get_route.start()
     loads = [
         pltpu.make_async_copy(mem.at[:, :, columns], own, in_sem.at[0]),
         pltpu.make_async_copy(mem, full, in_sem.at[1]),
         pltpu.make_async_copy(wk, wts.at[:, 0:COLS], in_sem.at[2]),
         pltpu.make_async_copy(wv, wts.at[:, COLS : 2 * COLS], in_sem.at[3]),
         pltpu.make_async_copy(wo, wout, in_sem.at[4]),
+        pltpu.make_async_copy(lengths_in, lengths, in_sem.at[7]),
+        pltpu.make_async_copy(query_in, query, in_sem.at[8]),
+        pltpu.make_async_copy(hidden_in, hidden, in_sem.at[9]),
     ]
     for load in loads:
         load.start()
 
     barrier = pltpu.get_barrier_semaphore()
 
-    def greet(k):
+    for k in range(NDP - 1, 0, -1):
         pl.semaphore_signal(barrier, inc=1, device_id=(peer(k), head), device_id_type=MESH)
-
-    each(1, NDP, greet)
     for step in range(1, NHEAD):
-        pl.semaphore_signal(barrier, inc=1, device_id=(dp, (head + step) % NHEAD), device_id_type=MESH)
-
+        pl.semaphore_signal(barrier, inc=1, device_id=(dp, lax.rem(head + step, NHEAD)), device_id_type=MESH)
+
+    get_route.wait()
     to_home = [route[0, j] for j in range(slots)]
 
-    def look_up(k):
+    for k in range(NDP):
         home = peer(k)
-        index, cell = jnp.int32(0), jnp.int32(-1)
+        index = jnp.int32(0)
         for j in range(slots):
-            hit = to_home[j] == home
-            index = jnp.where(hit, j, index)
-            cell = jnp.where(hit, route[1, j], cell)
+            index = jnp.where(to_home[j] == home, j, index)
         home_of[k] = index
-        tag_out[k] = jnp.full((1, 128), cell, jnp.int32)
-
-    each(0, NDP, look_up)
-    tags[0] = tag_out[0]
 
     loads[0].wait()
 
-    def fill(k):
+    for k in range(DIRECT, NDP):
         packed[k - DIRECT] = own[home_of[k]]
-
-    each(DIRECT, NDP, fill)
     pl.semaphore_wait(barrier, NDP - 1 + NHEAD - 1)
 
     def rows_of(g):
@@ -128,13 +127,22 @@
             send_sem=d_send.at[k], recv_sem=d_recv.at[k],
             device_id=(peer(k), head), device_id_type=MESH)
 
-    each(DIRECT, NDP, lambda k: a_copy(k).start())
+    for k in range(DIRECT, NDP):
+        a_copy(k).start()
+
+    rows_k = lax.broadcasted_iota(jnp.int32, (NDP, 1, 128), 0)
+    offset_z, offset_y = slot_offset(rows_k)
+    homes = ((z + offset_z) % ZN) * YN + (y + offset_y) % YN
+    cell = jnp.full((NDP, 1, 128), -1, jnp.int32)
+    for j in range(slots):
+        cell = jnp.where(homes == to_home[j], route[1, j], cell)
+    tag_out[...] = cell
+    tags[0] = cell[0]
+    for k in range(1, NDP):
+        t_copy(k).start()
 
     def project(rows):
         return jnp.dot(rows, wts[...], preferred_element_type=F32).astype(BF16)
-
-    for load in loads[1:4]:
-        load.wait()
 
     def direct_group(g):
         base = g * GROUP
@@ -142,10 +150,6 @@
         kv_out[pl.ds(base, GROUP)] = project(rows).reshape(GROUP, BLOCK, 2 * COLS)
         for i in range(GROUP):
             pl.when(base + i > 0)(lambda k=base + i: d_copy(k).start())
-
-    each(0, DIRECT // GROUP, direct_group)
-    kv[0] = kv_out[0]
-    each(1, NDP, lambda k: t_copy(k).start())
 
     def head_copy(piece, group, target, send, recv):
         where = pool.at[piece, rows_of(group), :]
@@ -193,9 +197,16 @@
         kv[pl.ds(DIRECT + g * GROUP, GROUP)] = project(rows).reshape(GROUP, BLOCK, 2 * COLS)
 
     def round_of(t):
+        def weights():
+            for load in loads[1:]:
+                load.wait()
+
+        pl.when(t == EARLY)(weights)
         for late, stage in enumerate((stage_own, stage_forward, stage_core, stage_project)):
             g = t - late * LAG
             pl.when((g >= 0) & (g < NGROUP))(functools.partial(stage, g))
+        n = t - EARLY
+        pl.when((n >= 0) & (n < DIRECT // GROUP))(lambda: direct_group(n))
 
     each(0, NGROUP + 2 * LAG, round_of)
 
@@ -207,6 +218,7 @@
     to_scalars.start()
 
     each(NGROUP + 2 * LAG, NGROUP + 3 * LAG, round_of)
+    kv[0] = kv_out[0]
     each(1, DIRECT, lambda k: d_copy(k).wait_recv())
     to_scalars.wait()
 
@@ -240,13 +252,12 @@
     for r in range(requests):
         mixed = jnp.dot(att[r * 8 : (r + 1) * 8, :], value_grid[r], preferred_element_type=F32)
         ctx[r : r + 1, :] = jnp.sum(jnp.where(own_head, mixed, 0.0), axis=0, keepdims=True)
-    loads[4].wait()
     summed = jnp.dot(ctx[...].astype(BF16), wout[...], preferred_element_type=F32)
     for p in range(NHEAD):
         partial[p] = summed[:, p * COLS : (p + 1) * COLS]
 
     def s_copy(step):
-        other = (head + step) % NHEAD
+        other = lax.rem(head + step, NHEAD)
         return pltpu.make_async_remote_copy(
             src_ref=partial.at[other], dst_ref=parts.at[step],
             send_sem=s_send.at[step], recv_sem=s_recv.at[step],
@@ -272,24 +283,49 @@
     for step in range(1, NHEAD):
         s_copy(step).wait_recv()
         total = total + parts[step]
-    new_hidden[...] = (hidden[...].astype(F32) + total[0:requests, :]).astype(BF16)
+    summed_hidden[...] = (hidden[...].astype(F32) + total[0:requests, :]).astype(BF16)
+    outs.append(pltpu.make_async_copy(summed_hidden, new_hidden, in_sem.at[10]))
+    outs[-1].start()
     for step in range(1, NHEAD):
         s_copy(step).wait_send()
     for copy in outs:
         copy.wait()
 
 
+def hand_on_kernel(hidden_in, keys_in, values_in, hidden, keys, values, staged, small, in_sem, out_sem, small_sem):
+    requests = keys.shape[0]
+    steps = [(i, r) for r in range(requests) for i in range(2)]
+    takes, gives = [], []
+    for i, r in steps:
+        source, target = (keys_in, keys) if i == 0 else (values_in, values)
+        takes.append(pltpu.make_async_copy(source.at[r], staged.at[i, r], in_sem.at[i, r]))
+        gives.append(pltpu.make_async_copy(staged.at[i, r], target.at[r], out_sem.at[i, r]))
+    get_small = pltpu.make_async_copy(hidden_in, small, small_sem.at[0])
+    put_small = pltpu.make_async_copy(small, hidden, small_sem.at[1])
+    get_small.start()
+    for take in takes:
+        take.start()
+    get_small.wait()
+    put_small.start()
+    for take, give in zip(takes, gives):
+        take.wait()
+        give.start()
+    for give in gives:
+        give.wait()
+    put_small.wait()
+
+
 def shards(memory, block_route, enc_len, w_key, w_value, dec_query, dec_hidden, w_out):
     slots, depth, requests = block_route.shape[1], memory.shape[1], enc_len.shape[0]
     span = MAXB * BLOCK
     dma, bufs = pltpu.SemaphoreType.DMA, pltpu.VMEM
-    vmem, smem, anywhere = (pl.BlockSpec(memory_space=s) for s in (pltpu.VMEM, pltpu.SMEM, pl.ANY))
+    anywhere = pl.BlockSpec(memory_space=pl.ANY)
     grid = jax.ShapeDtypeStruct((requests, span, COLS), BF16)
-    return pl.pallas_call(
+    results = pl.pallas_call(
         whole_kernel,
         out_shape=(jax.ShapeDtypeStruct(dec_hidden.shape, BF16), grid, grid),
-        in_specs=[smem, smem, vmem, vmem, anywhere, anywhere, anywhere, anywhere],
-        out_specs=(vmem, anywhere, anywhere),
+        in_specs=[anywhere] * 8,
+        out_specs=(anywhere, anywhere, anywhere),
         scratch_shapes=[
             bufs((slots, BLOCK, COLS), BF16),
             bufs((slots, BLOCK, depth), BF16),
@@ -311,7 +347,12 @@
             bufs((NHEAD, 8, COLS), F32),
             pltpu.SMEM((NDP,), jnp.int32),
             pltpu.SMEM((1, 128), jnp.int32),
-            dma((6,)),
+            pltpu.SMEM(block_route.shape, jnp.int32),
+            pltpu.SMEM(enc_len.shape, jnp.int32),
+            bufs(dec_query.shape, BF16),
+            bufs(dec_hidden.shape, BF16),
+            bufs(dec_hidden.shape, BF16),
+            dma((11,)),
             *[dma((NDP,)) for _ in range(6)],
             *[dma((NGROUP,)) for _ in range(6)],
             dma((4, NGROUP)),
@@ -328,6 +369,21 @@
         ),
         name="whole",
     )(block_route, enc_len, dec_query, dec_hidden, memory.reshape(slots, BLOCK, depth), w_key, w_value, w_out)
+    return pl.pallas_call(
+        hand_on_kernel,
+        out_shape=tuple(jax.ShapeDtypeStruct(a.shape, a.dtype) for a in results),
+        in_specs=[anywhere] * 3,
+        out_specs=(anywhere,) * 3,
+        scratch_shapes=[
+            bufs((2, requests, span, COLS), BF16),
+            bufs(dec_hidden.shape, BF16),
+            dma((2, requests)),
+            dma((2, requests)),
+            dma((2,)),
+        ],
+        compiler_params=pltpu.CompilerParams(vmem_limit_bytes=56 * 2**20),
+        name="hand_on",
+    )(*results)
 
 
 def solution(mesh):

time: 88.8 us -> 83.6 us (0.941)
  local copies, waits for them, and re-layouts: 5.19 us -> 0 us
  Pallas kernels: 82 us -> 82.9 us
    unnamed x5 -> x0, local copies, waits for them, and re-layouts: 5.19 us -> none
    pallas_call x0 -> x1, Pallas kernels: none -> 3.42 us  [shards(): pl.pallas_call(hand_on_kernel, out_shape=tuple((jax.ShapeDtypeStruct(a.sh...]
    pallas_call x1, Pallas kernels: 82 us -> 79.4 us  [shards(): pl.pallas_call(whole_kernel, out_shape=(jax.ShapeDtypeStruct(dec_hidden.s...]
where the time goes in v3:
time: 83.6 us; the launch traced here: 83.5 us
  Pallas kernels  82.9 us (99%)
    pallas_call x1, Pallas kernels, shards(): pl.pallas_call(whole_kernel, out_shape=(jax.ShapeDtypeStruct(dec_hidden.s...  79.4 us
    pallas_call x1, Pallas kernels, shards(): pl.pallas_call(hand_on_kernel, out_shape=tuple((jax.ShapeDtypeStruct(a.sh...  3.42 us

profile of v3, /device:TPU:1, one launch (start us, length us, event | category | flops | bytes accessed | tf_op | source)
XLA Modules:
  0.0 83.5 jit_solution(9220025665755478568)
XLA Ops:
  0.6 79.4 %whole.1 = (bf16[6,256]{1,0:T(8,128)(2,1)}, bf16[6,512,256]{2,1,0:T(8,128)(2,1)}, bf16[6,512,256]{2,1,0:T(8,128)(2,1)}) custom-call(s32[2,15]{1,0:T(2,128)} %route_in.1, s32[6]{0:T(128)} %lengths_in.1, bf16[6,256]{1,0:T(8,128)(2,1)} %query_in.1, bf16[6,256]{1,0:T(8,128)(2,1)} %hidden_in.1, bf16[15,128,2048]{2,1,0:T(8,128)(2,1)} %bitcast.1, ...), custom_call_target="tpu_custom_call" | custom-call | flops 8589934592 | bytes 25165824 | tf_op jit(solution)/shard_map/whole/pallas_call | solution.py:324
  80.1 3.4 %hand_on.1 = (bf16[6,256]{1,0:T(8,128)(2,1)}, bf16[6,512,256]{2,1,0:T(8,128)(2,1)}, bf16[6,512,256]{2,1,0:T(8,128)(2,1)}) custom-call(bf16[6,256]{1,0:T(8,128)(2,1)} %get-tuple-element.6.hidden_in, bf16[6,512,256]{2,1,0:T(8,128)(2,1)} %get-tuple-element.7.keys_in, bf16[6,512,256]{2,1,0:T(8,128)(2,1)} %get-tuple-element.8.values_in), custom_call_target="tpu_custom_call" | custom-call | tf_op jit(solution)/shard_map/hand_on/pallas_call | solution.py:372

commit v4 on v3

--- a/solution.py
+++ b/solution.py
@@ -13,11 +13,12 @@
 ZN, YN, XN, CN = 8, 4, 4, 2
 NDP, NHEAD = ZN * YN, XN * CN
 COLS = 256
-DIRECT = 10
-GROUP = 2
-LAG = 1
-
-EARLY = 3
+DIRECT = 11
+GROUP = 1
+LAG = 3
+
+SEND = 16
+EARLY = 4
 NMEM = NDP - DIRECT
 NGROUP = NMEM // GROUP
 MESH = pl.DeviceIdType.MESH
@@ -148,8 +149,6 @@
         base = g * GROUP
         rows = jnp.concatenate([full[home_of[base + i]] for i in range(GROUP)], axis=0)
         kv_out[pl.ds(base, GROUP)] = project(rows).reshape(GROUP, BLOCK, 2 * COLS)
-        for i in range(GROUP):
-            pl.when(base + i > 0)(lambda k=base + i: d_copy(k).start())
 
     def head_copy(piece, group, target, send, recv):
         where = pool.at[piece, rows_of(group), :]
@@ -205,6 +204,11 @@
         for late, stage in enumerate((stage_own, stage_forward, stage_core, stage_project)):
             g = t - late * LAG
             pl.when((g >= 0) & (g < NGROUP))(functools.partial(stage, g))
+        def send_direct():
+            for k in range(1, DIRECT):
+                d_copy(k).start()
+
+        pl.when(t == SEND)(send_direct)
         n = t - EARLY
         pl.when((n >= 0) & (n < DIRECT // GROUP))(lambda: direct_group(n))
 

time: 83.6 us -> 80.8 us (0.967)
  Pallas kernels: 82.9 us -> 80.1 us
    pallas_call x1, Pallas kernels: 79.4 us -> 76.7 us  [shards(): pl.pallas_call(whole_kernel, out_shape=(jax.ShapeDtypeStruct(dec_hidden.s...]
where the time goes in v4:
time: 80.8 us; the launch traced here: 80.7 us
  Pallas kernels  80.1 us (99%)
    pallas_call x1, Pallas kernels, shards(): pl.pallas_call(whole_kernel, out_shape=(jax.ShapeDtypeStruct(dec_hidden.s...  76.7 us
    pallas_call x1, Pallas kernels, shards(): pl.pallas_call(hand_on_kernel, out_shape=tuple((jax.ShapeDtypeStruct(a.sh...  3.42 us

profile of v4, /device:TPU:1, one launch (start us, length us, event | category | flops | bytes accessed | tf_op | source)
XLA Modules:
  0.0 80.7 jit_solution(13503474572195252521)
XLA Ops:
  0.6 76.7 %whole.1 = (bf16[6,256]{1,0:T(8,128)(2,1)}, bf16[6,512,256]{2,1,0:T(8,128)(2,1)}, bf16[6,512,256]{2,1,0:T(8,128)(2,1)}) custom-call(s32[2,15]{1,0:T(2,128)} %route_in.1, s32[6]{0:T(128)} %lengths_in.1, bf16[6,256]{1,0:T(8,128)(2,1)} %query_in.1, bf16[6,256]{1,0:T(8,128)(2,1)} %hidden_in.1, bf16[15,128,2048]{2,1,0:T(8,128)(2,1)} %bitcast.1, ...), custom_call_target="tpu_custom_call" | custom-call | flops 8589934592 | bytes 25165824 | tf_op jit(solution)/shard_map/whole/pallas_call | solution.py:328
  77.3 3.4 %hand_on.1 = (bf16[6,256]{1,0:T(8,128)(2,1)}, bf16[6,512,256]{2,1,0:T(8,128)(2,1)}, bf16[6,512,256]{2,1,0:T(8,128)(2,1)}) custom-call(bf16[6,256]{1,0:T(8,128)(2,1)} %get-tuple-element.6.hidden_in, bf16[6,512,256]{2,1,0:T(8,128)(2,1)} %get-tuple-element.7.keys_in, bf16[6,512,256]{2,1,0:T(8,128)(2,1)} %get-tuple-element.8.values_in), custom_call_target="tpu_custom_call" | custom-call | tf_op jit(solution)/shard_map/hand_on/pallas_call | solution.py:376

commit v5 on v4

--- a/solution.py
+++ b/solution.py
@@ -201,7 +201,7 @@
                 load.wait()
 
         pl.when(t == EARLY)(weights)
-        for late, stage in enumerate((stage_own, stage_forward, stage_core, stage_project)):
+        for late, stage in ((1, stage_forward), (2, stage_core), (0, stage_own), (3, stage_project)):
             g = t - late * LAG
             pl.when((g >= 0) & (g < NGROUP))(functools.partial(stage, g))
         def send_direct():

time: 80.8 us -> 81.1 us (level)
  no operation moved by 1% of the time
where the time goes in v5:
time: 81.1 us; the launch traced here: 81 us
  Pallas kernels  80.4 us (99%)
    pallas_call x1, Pallas kernels, shards(): pl.pallas_call(whole_kernel, out_shape=(jax.ShapeDtypeStruct(dec_hidden.s...  77 us
    pallas_call x1, Pallas kernels, shards(): pl.pallas_call(hand_on_kernel, out_shape=tuple((jax.ShapeDtypeStruct(a.sh...  3.42 us

profile of v5, /device:TPU:1, one launch (start us, length us, event | category | flops | bytes accessed | tf_op | source)
XLA Modules:
  0.0 81.0 jit_solution(5590803267392680166)
XLA Ops:
  0.6 77.0 %whole.1 = (bf16[6,256]{1,0:T(8,128)(2,1)}, bf16[6,512,256]{2,1,0:T(8,128)(2,1)}, bf16[6,512,256]{2,1,0:T(8,128)(2,1)}) custom-call(s32[2,15]{1,0:T(2,128)} %route_in.1, s32[6]{0:T(128)} %lengths_in.1, bf16[6,256]{1,0:T(8,128)(2,1)} %query_in.1, bf16[6,256]{1,0:T(8,128)(2,1)} %hidden_in.1, bf16[15,128,2048]{2,1,0:T(8,128)(2,1)} %bitcast.1, ...), custom_call_target="tpu_custom_call" | custom-call | flops 8589934592 | bytes 25165824 | tf_op jit(solution)/shard_map/whole/pallas_call | solution.py:328
  77.6 3.4 %hand_on.1 = (bf16[6,256]{1,0:T(8,128)(2,1)}, bf16[6,512,256]{2,1,0:T(8,128)(2,1)}, bf16[6,512,256]{2,1,0:T(8,128)(2,1)}) custom-call(bf16[6,256]{1,0:T(8,128)(2,1)} %get-tuple-element.6.hidden_in, bf16[6,512,256]{2,1,0:T(8,128)(2,1)} %get-tuple-element.7.keys_in, bf16[6,512,256]{2,1,0:T(8,128)(2,1)} %get-tuple-element.8.values_in), custom_call_target="tpu_custom_call" | custom-call | tf_op jit(solution)/shard_map/hand_on/pallas_call | solution.py:376
